TPU v7x, 32 devices: a whole 2x2x4 slice. The times are simulated.
32 devices in a mesh: rep: 8 (over z, y), shard: 4 (over x, core).
Axes of the slice: x: 2, y: 2, z: 4, core: 2. Of those that a mesh axis runs over, the one named last changes fastest.
Arguments:
- tokens: bfloat16 [8192, 1024], P(('rep', 'shard')), may hold values from -6 to 6
- segment_ids: int32 [8, 1024], P('rep'), may hold values from 0 to 4, as said below
- ln1_gain: bfloat16 [1024], P('shard'), may hold values from 0.099609375 to 1.8984375
- w_qkv: bfloat16 [1024, 3072], P('shard'), may hold values from -0.1875 to 0.1875
- w_out: bfloat16 [1024, 1024], P('shard'), may hold values from -1.5 to 1.5
- ln2_gain: bfloat16 [1024], P('shard'), may hold values from 0.099609375 to 1.8984375
- w_in: bfloat16 [1024, 5248], P('shard'), may hold values from -0.1875 to 0.1875
- w_down: bfloat16 [2624, 1024], P('shard'), may hold values from -0.125 to 0.125
- cotangent: bfloat16 [8192, 1024], P(('rep', 'shard')), may hold values from -6 to 6
Outputs:
- activations: bfloat16 [8192, 1024], P(('rep', 'shard'))
- input_grad: float32 [8192, 1024], P(('rep', 'shard'))
- ln1_grad: float32 [1024], P('shard')
- qkv_grad: float32 [1024, 3072], P('shard')
- out_grad: float32 [1024, 1024], P('shard')
- ln2_grad: float32 [1024], P('shard')
- in_grad: float32 [1024, 5248], P('shard')
- down_grad: float32 [2624, 1024], P('shard')
Inputs may be any that keep to these rules, and one draw needn't show every extreme that they name: `segment_ids`: along each packed sequence the numbers never fall; one document covers every position from some position under 256 to some position at or over 1024 - 255; the other documents lie before or after it.
All inputs are finite; a program needn't handle non-finite values.
Results may differ from a plain program's by a relative error of at most 0.018.
Values may be sent and summed in bfloat16 or wider, within the bound.
No kernel may reach another device: no remote copies, remote signals or barrier semaphores. Data moves between devices by JAX's collectives and lax.ppermute only.
A program may use at most 192 MiB of HBM per device.

v0:
```python
import math

import jax
import jax.numpy as jnp
from jax import lax
from jax.sharding import PartitionSpec as P

HEADS = 16
FF = 2624
WINDOW = 128


norm_epsilon = 1e-05
rope_base = 10000.0
masked_score = -1e30


def with_halo(x, sides, width):
    for axis, dim in sides:
        size, length = (lax.axis_size(axis), x.shape[dim])
        up = [(i, (i + 1) % size) for i in range(size - 1)]
        down = [(j, i) for i, j in up]
        last = lax.slice_in_dim(x, length - width, length, axis=dim)
        initial = lax.slice_in_dim(x, 0, width, axis=dim)
        before = lax.ppermute(last, axis, up)
        after = lax.ppermute(initial, axis, down)
        x = jnp.concatenate([before, x, after], axis=dim)
    return x


def apply_layer_norm(values):
    centred = values - jnp.mean(values, axis=-1, keepdims=True)
    scale_inv = lax.rsqrt(jnp.mean(centred * centred, axis=-1, keepdims=True) + norm_epsilon)
    return (centred * scale_inv, scale_inv)


def norm_backward(grad_hat, normed, scale_inv):
    return (
        grad_hat
        - jnp.mean(grad_hat, axis=-1, keepdims=True)
        - normed * jnp.mean(grad_hat * normed, axis=-1, keepdims=True)
    ) * scale_inv


def rope_tables(positions, head_dim):
    half_dim = head_dim // 2
    frequency = jnp.exp(
        -math.log(rope_base) * 2.0 * jnp.arange(half_dim, dtype=jnp.float32) / head_dim
    )
    angles = positions.astype(jnp.float32)[:, None] * frequency[None, :]
    return (jnp.cos(angles)[:, None, :], jnp.sin(angles)[:, None, :])


def rotate(values, cosine_table, sine_table):
    half_dim = values.shape[-1] // 2
    front_half = values[..., :half_dim]
    back_half = values[..., half_dim:]
    return jnp.concatenate(
        [
            front_half * cosine_table - back_half * sine_table,
            back_half * cosine_table + front_half * sine_table,
        ],
        axis=-1,
    )


def unrotate(grads, cosine_table, sine_table):
    half_dim = grads.shape[-1] // 2
    front_half = grads[..., :half_dim]
    back_half = grads[..., half_dim:]
    return jnp.concatenate(
        [
            front_half * cosine_table + back_half * sine_table,
            back_half * cosine_table - front_half * sine_table,
        ],
        axis=-1,
    )


def geglu(gate_part, linear_part):
    return jax.nn.gelu(gate_part, approximate=False) * linear_part


def replica_total(gain_part, first_part, second_part):
    gain_whole = lax.psum(gain_part, "rep")
    first_share, second_share = (
        lax.psum_scatter(
            first_part.astype(jnp.bfloat16), "rep", scatter_dimension=1, tiled=True
        ).astype(jnp.float32),
        lax.psum_scatter(
            second_part.astype(jnp.bfloat16), "rep", scatter_dimension=1, tiled=True
        ).astype(jnp.float32),
    )
    first_whole, second_whole = (
        lax.all_gather(first_share.astype(jnp.bfloat16), "rep", axis=1, tiled=True).astype(
            first_share.dtype
        ),
        lax.all_gather(second_share.astype(jnp.bfloat16), "rep", axis=1, tiled=True).astype(
            second_share.dtype
        ),
    )
    return (gain_whole, first_whole, second_whole)


def shards(tokens, segment_ids, ln1_gain, w_qkv, w_out, ln2_gain, w_in, w_down, cotangent):
    tok_rows, model_width = tokens.shape
    head_dim = model_width // HEADS
    half_width = WINDOW // 2
    key_rows = tok_rows + 2 * half_width
    row_start = lax.axis_index("shard") * tok_rows
    seq_row = segment_ids[0]
    padded_ids = jnp.pad(seq_row, (half_width, half_width), constant_values=-1)
    key_ids = lax.dynamic_slice_in_dim(padded_ids, row_start, key_rows)
    query_ids = lax.dynamic_slice_in_dim(seq_row, row_start, tok_rows)
    query_pos = row_start + jnp.arange(tok_rows, dtype=jnp.int32)
    key_pos = row_start - half_width + jnp.arange(key_rows, dtype=jnp.int32)
    allowed = (query_ids[:, None] == key_ids[None, :]) & (
        jnp.abs(query_pos[:, None] - key_pos[None, :]) <= half_width
    )
    cosine_table, sine_table = rope_tables(query_pos, head_dim)
    score_scale = 1.0 / math.sqrt(head_dim)
    first_norm_gain, qkv_full, out_full = (
        lax.all_gather(ln1_gain, "shard", axis=0, tiled=True),
        lax.all_gather(w_qkv, "shard", axis=0, tiled=True),
        lax.all_gather(w_out, "shard", axis=0, tiled=True),
    )
    layer_inputs = tokens.astype(jnp.float32)
    first_centred_scaled, first_inverse_deviation = apply_layer_norm(layer_inputs)
    first_normalized = (first_centred_scaled * first_norm_gain.astype(jnp.float32)).astype(
        jnp.bfloat16
    )
    qkv = jnp.dot(first_normalized, qkv_full, preferred_element_type=jnp.float32)
    query_low = rotate(
        qkv[:, :model_width].reshape(tok_rows, HEADS, head_dim), cosine_table, sine_table
    ).astype(jnp.bfloat16)
    key_low = rotate(
        qkv[:, model_width : 2 * model_width].reshape(tok_rows, HEADS, head_dim),
        cosine_table,
        sine_table,
    ).astype(jnp.bfloat16)
    value_low = qkv[:, 2 * model_width :].astype(jnp.bfloat16)
    key_value = jnp.stack([key_low.reshape(tok_rows, model_width), value_low])
    extended = with_halo(key_value, (("shard", 1),), half_width)
    keys_ext = extended[0].reshape(key_rows, HEADS, head_dim)
    values_ext = extended[1].reshape(key_rows, HEADS, head_dim)

    def masked_scores():
        raw_scores = (
            jnp.einsum("qhd,khd->hqk", query_low, keys_ext, preferred_element_type=jnp.float32)
            * score_scale
        )
        return jnp.where(allowed[None, :, :], raw_scores, masked_score)

    scores = masked_scores()
    maxima = jnp.max(scores, axis=-1, keepdims=True)
    log_totals = maxima + jnp.log(jnp.sum(jnp.exp(scores - maxima), axis=-1, keepdims=True))
    attn_probs = jnp.exp(scores - log_totals)
    attended = jnp.einsum(
        "hqk,khd->qhd",
        attn_probs.astype(jnp.bfloat16),
        values_ext,
        preferred_element_type=jnp.float32,
    )
    attended_low = attended.reshape(tok_rows, model_width).astype(jnp.bfloat16)
    first_hidden_state = layer_inputs + jnp.dot(
        attended_low, out_full, preferred_element_type=jnp.float32
    )
    second_norm_gain, in_full, down_full = (
        lax.all_gather(ln2_gain, "shard", axis=0, tiled=True),
        lax.all_gather(w_in, "shard", axis=0, tiled=True),
        lax.all_gather(w_down, "shard", axis=0, tiled=True),
    )
    second_centred_scaled, second_inverse_deviation = apply_layer_norm(first_hidden_state)
    second_normalized = (second_centred_scaled * second_norm_gain.astype(jnp.float32)).astype(
        jnp.bfloat16
    )
    up_proj = jnp.dot(second_normalized, in_full, preferred_element_type=jnp.float32)
    act_value, geglu_pull = jax.vjp(geglu, up_proj[:, :FF], up_proj[:, FF:])
    act_low = act_value.astype(jnp.bfloat16)
    mlp_value = jnp.dot(act_low, down_full, preferred_element_type=jnp.float32)
    output = (first_hidden_state + mlp_value).astype(jnp.bfloat16)
    grad_out = cotangent.astype(jnp.float32)
    grad_act = jnp.einsum("td,fd->tf", cotangent, down_full, preferred_element_type=jnp.float32)
    grad_gate, grad_linear = geglu_pull(grad_act)
    grad_up = jnp.concatenate([grad_gate, grad_linear], axis=1).astype(jnp.bfloat16)
    second_normalized_gradient = jnp.einsum(
        "tf,df->td", grad_up, in_full, preferred_element_type=jnp.float32
    )
    second_gain_slice = jnp.sum(second_normalized_gradient * second_centred_scaled, axis=0)
    grad_hidden = grad_out + norm_backward(
        second_normalized_gradient * second_norm_gain.astype(jnp.float32),
        second_centred_scaled,
        second_inverse_deviation,
    )
    grad_proj = grad_hidden.astype(jnp.bfloat16)
    grad_attended = jnp.einsum("td,ad->ta", grad_proj, out_full, preferred_element_type=jnp.float32)
    grad_attended = grad_attended.astype(jnp.bfloat16).reshape(tok_rows, HEADS, head_dim)
    attn_probs = jnp.exp(masked_scores() - log_totals)
    grad_probs = jnp.einsum(
        "qhd,khd->hqk", grad_attended, values_ext, preferred_element_type=jnp.float32
    )
    delta_rows = jnp.sum(attn_probs * grad_probs, axis=-1, keepdims=True)
    grad_scores = (attn_probs * (grad_probs - delta_rows)).astype(jnp.bfloat16)
    grad_query = (
        jnp.einsum("hqk,khd->qhd", grad_scores, keys_ext, preferred_element_type=jnp.float32)
        * score_scale
    )
    grad_keys = (
        jnp.einsum("hqk,qhd->khd", grad_scores, query_low, preferred_element_type=jnp.float32)
        * score_scale
    )
    grad_values = jnp.einsum(
        "hqk,qhd->khd",
        attn_probs.astype(jnp.bfloat16),
        grad_attended,
        preferred_element_type=jnp.float32,
    )
    pair_grad = jnp.stack(
        [grad_keys.reshape(key_rows, model_width), grad_values.reshape(key_rows, model_width)]
    )
    rim_parts = jnp.concatenate(
        [pair_grad[:, :half_width], pair_grad[:, half_width + tok_rows :]], axis=1
    )
    incoming = with_halo(rim_parts.astype(jnp.bfloat16), (("shard", 1),), half_width).astype(
        rim_parts.dtype
    )
    own_grad = pair_grad[:, half_width : half_width + tok_rows]
    own_grad = own_grad.at[:, :half_width].add(incoming[:, :half_width])
    own_grad = own_grad.at[:, tok_rows - half_width :].add(incoming[:, 3 * half_width :])
    grad_q = unrotate(grad_query, cosine_table, sine_table).reshape(tok_rows, model_width)
    grad_k = unrotate(
        own_grad[0].reshape(tok_rows, HEADS, head_dim), cosine_table, sine_table
    ).reshape(tok_rows, model_width)
    grad_qkv = jnp.concatenate([grad_q, grad_k, own_grad[1]], axis=1).astype(jnp.bfloat16)
    first_normalized_gradient = jnp.einsum(
        "te,de->td", grad_qkv, qkv_full, preferred_element_type=jnp.float32
    )
    first_gain_slice = jnp.sum(first_normalized_gradient * first_centred_scaled, axis=0)
    grad_input = grad_hidden + norm_backward(
        first_normalized_gradient * first_norm_gain.astype(jnp.float32),
        first_centred_scaled,
        first_inverse_deviation,
    )
    columns = (
        lax.all_to_all(first_normalized, "shard", split_axis=1, concat_axis=0, tiled=True),
        lax.all_to_all(attended_low, "shard", split_axis=1, concat_axis=0, tiled=True),
        lax.all_to_all(second_normalized, "shard", split_axis=1, concat_axis=0, tiled=True),
        lax.all_to_all(act_low, "shard", split_axis=1, concat_axis=0, tiled=True),
    )
    grouped = (
        lax.all_gather(grad_qkv, "shard", axis=0, tiled=True),
        lax.all_gather(grad_proj, "shard", axis=0, tiled=True),
        lax.all_gather(grad_up, "shard", axis=0, tiled=True),
        lax.all_gather(cotangent, "shard", axis=0, tiled=True),
    )
    qkv_total = jnp.einsum("td,te->de", columns[0], grouped[0], preferred_element_type=jnp.float32)
    out_total = jnp.einsum("ta,td->ad", columns[1], grouped[1], preferred_element_type=jnp.float32)
    in_total = jnp.einsum("td,tf->df", columns[2], grouped[2], preferred_element_type=jnp.float32)
    down_total = jnp.einsum("tf,td->fd", columns[3], grouped[3], preferred_element_type=jnp.float32)
    gain_one_total, gain_two_total = (
        lax.psum_scatter(first_gain_slice, "shard", scatter_dimension=0, tiled=True),
        lax.psum_scatter(second_gain_slice, "shard", scatter_dimension=0, tiled=True),
    )
    gain_two_total, in_total, down_total = replica_total(gain_two_total, in_total, down_total)
    gain_one_total, qkv_total, out_total = replica_total(gain_one_total, qkv_total, out_total)
    return (
        output,
        grad_input,
        gain_one_total,
        qkv_total,
        out_total,
        gain_two_total,
        in_total,
        down_total,
    )


def solution(mesh):
    return jax.shard_map(
        shards,
        mesh=mesh,
        in_specs=(
            P(("rep", "shard"), None),
            P("rep", None),
            P("shard"),
            P("shard", None),
            P("shard", None),
            P("shard"),
            P("shard", None),
            P("shard", None),
            P(("rep", "shard"), None),
        ),
        out_specs=(
            P(("rep", "shard"), None),
            P(("rep", "shard"), None),
            P("shard"),
            P("shard", None),
            P("shard", None),
            P("shard"),
            P("shard", None),
            P("shard", None),
        ),
        check_vma=False,
    )
```

profile of v0, /device:TPU:0, one launch (start us, length us, event | category | flops | bytes accessed | tf_op | source)
XLA Modules:
  0.0 891.4 jit_solution(14228811978769375009)
XLA Ops:
  11.2 6.0 all-gather
  17.8 40.9 %all-gather.14.cloned.1.call-done = bf16[1024,3072]{1,0:T(8,128)(2,1)} async-done(((bf16[256,3072]{1,0:T(8,128)(2,1)}), bf16[1024,3072]{1,0:T(8,128)(2,1)}) %all-gather.14.cloned.1.call-update) | async-done | bytes 6291472 | tf_op jit(solution)/shard_map/all_gather | solution.py:124
  75.1 9.9 %all-gather.1 = bf16[4,1,256]{2,1,0:T(2,128)(2,1)S(1)} all-gather(bf16[1,1,256]{2,1,0:T(2,128)(2,1)S(1)} %reshape.303), channel_id=1, replica_groups=mesh['rep'=8,'shard'=4] {'shard'}, dimensions={0}, use_global_device_ids=true | all-gather | bytes 2560 | tf_op jit(solution)/shard_map/all_gather | solution.py:169
  91.2 5.4 convolution_convert_fusion.5
  100.0 58.6 %all-gather.18.cloned.1.call-done = bf16[1024,5248]{1,0:T(8,128)(2,1)} async-done(((bf16[256,5248]{1,0:T(8,128)(2,1)}), bf16[1024,5248]{1,0:T(8,128)(2,1)}) %all-gather.18.cloned.1.call-update) | async-done | bytes 10747920 | tf_op jit(solution)/shard_map/all_gather | solution.py:170
  158.7 8.8 fusion.50
  167.5 33.8 %all-gather.20.cloned.1.call-done = bf16[2624,1024]{1,0:T(8,128)(2,1)} async-done(((bf16[656,1024]{1,0:T(8,128)(2,1)}), bf16[2624,1024]{1,0:T(8,128)(2,1)}) %all-gather.20.cloned.1.call-update) | async-done | bytes 5373968 | tf_op jit(solution)/shard_map/all_gather | solution.py:171
  201.3 11.2 %add_convert_fusion = (bf16[256,2624]{1,0:T(8,128)(2,1)S(1)}, f32[256,2624]{1,0:T(8,128)S(1)}, f32[256,2624]{1,0:T(8,128)S(1)}) fusion(f32[256,5248]{1,0:T(8,128)} %fusion.50, bf16[256,1024]{1,0:T(8,128)(2,1)S(1)} %copy-done.26, bf16[2624,1024]{1,0:T(8,128)(2,1)} %all-gather.20.cloned.1.call-done), kind=kOutput, calls=%fused_computation.18 | convolution fusion | flops 1424769024 | bytes 17989632 | tf_op jit(solution)/shard_map/td,fd->tf/dot_general | solution.py:183
  216.6 7.8 multiply_reduce_fusion.1
  231.4 4.7 fusion.32
  251.8 8.7 scatter-add.6
  263.3 8.7 scatter-add.9
  279.1 36.7 %all_to_all.73 = bf16[256,4,656]{0,2,1:T(8,128)(2,1)S(1)} all-to-all(bf16[256,4,656]{0,2,1:T(8,128)(2,1)} %bitcast.102), channel_id=1, replica_groups=mesh['rep'=8,'shard'=4] {'shard'}, dimensions={1} | all-to-all | bytes 2686976 | tf_op jit(solution)/shard_map/all_to_all | solution.py:248
  324.5 17.5 %all_to_all.74 = bf16[256,4,256]{2,0,1:T(8,128)(2,1)S(1)} all-to-all(bf16[256,4,256]{2,0,1:T(8,128)(2,1)S(1)} %bitcast.114), channel_id=1, replica_groups=mesh['rep'=8,'shard'=4] {'shard'}, dimensions={1} | all-to-all | bytes 1048576 | tf_op jit(solution)/shard_map/all_to_all | solution.py:245
  346.4 5.8 convolution_convert_fusion.1
  355.0 16.9 %all_to_all.75 = bf16[256,4,256]{2,0,1:T(8,128)(2,1)S(1)} all-to-all(bf16[256,4,256]{2,0,1:T(8,128)(2,1)S(1)} %bitcast.115), channel_id=1, replica_groups=mesh['rep'=8,'shard'=4] {'shard'}, dimensions={1} | all-to-all | bytes 1048576 | tf_op jit(solution)/shard_map/all_to_all | solution.py:247
  371.8 53.9 %all-gather.28.cloned.1.call-done = bf16[1024,5248]{1,0:T(8,128)(2,1)} async-done(((bf16[256,5248]{1,0:T(8,128)(2,1)}), bf16[1024,5248]{1,0:T(8,128)(2,1)}) %all-gather.28.cloned.1.call-update) | async-done | bytes 10747920 | tf_op jit(solution)/shard_map/all_gather | solution.py:253
  425.7 9.9 %convolution_convert_fusion = bf16[256,5248]{0,1:T(8,128)(2,1)} fusion(bf16[1024,256]{1,0:T(8,128)(2,1)S(1)} %bitcast.125, bf16[1024,5248]{1,0:T(8,128)(2,1)} %all-gather.28.cloned.1.call-done), kind=kOutput, calls=%fused_computation | convolution fusion | flops 2752806912 | bytes 13959168 | tf_op jit(solution)/shard_map/td,tf->df/dot_general | solution.py:258
  436.9 17.2 %all_to_all.76 = bf16[256,4,256]{2,0,1:T(8,128)(2,1)S(1)} all-to-all(bf16[256,4,256]{2,0,1:T(8,128)(2,1)S(1)} %copy.54), channel_id=1, replica_groups=mesh['rep'=8,'shard'=4] {'shard'}, dimensions={1} | all-to-all | bytes 1048576 | tf_op jit(solution)/shard_map/all_to_all | solution.py:246
  459.7 64.9 %reduce-scatter.17.cloned.1.call-done = bf16[128,656]{1,0:T(8,128)(2,1)} async-done(((bf16[1024,656]{1,0:T(8,128)(2,1)}), bf16[128,656]{1,0:T(8,128)(2,1)}) %reduce-scatter.17.cloned.1.call-update) | async-done | bytes 167952
  526.4 66.3 %reduce-scatter.13.cloned.1.call-done = bf16[384,256]{1,0:T(8,128)(2,1)} async-done(((bf16[3072,256]{1,0:T(8,128)(2,1)}), bf16[384,256]{1,0:T(8,128)(2,1)}) %reduce-scatter.13.cloned.1.call-update) | async-done | bytes 196624
  594.6 71.8 %reduce-scatter.11.cloned.1.call-done = bf16[256,656]{0,1:T(8,128)(2,1)} async-done(((bf16[256,5248]{0,1:T(8,128)(2,1)}), bf16[256,656]{0,1:T(8,128)(2,1)}) %reduce-scatter.11.cloned.1.call-update) | async-done | bytes 335888 | tf_op jit(solution)/shard_map/reduce_scatter | solution.py:87
  667.8 5.1 fusion.12
  673.0 5.0 fusion.24
  678.0 5.9 all-reduce.4
  684.1 20.6 %all-reduce.3 = (f32[256]{0:T(256)}, f32[256]{0:T(256)}) all-reduce(f32[256]{0:T(256)S(1)} %dynamic-slice.18, f32[256]{0:T(256)S(1)} %dynamic-slice.20), channel_id=1, replica_groups=mesh['rep'=8,'shard'=4] {'rep'}, use_global_device_ids=true, to_apply=%region_13.14 | all-reduce | flops 512 | bytes 4096 | tf_op jit(solution)/shard_map/psum | solution.py:85
  706.0 25.2 %reduce-scatter.15.cloned.1.call-done = bf16[128,256]{1,0:T(8,128)(2,1)} async-done(((bf16[1024,256]{1,0:T(8,128)(2,1)}), bf16[128,256]{1,0:T(8,128)(2,1)}) %reduce-scatter.15.cloned.1.call-update) | async-done | bytes 65552
  732.2 28.3 %all_gather.51 = bf16[256,1024]{1,0:T(8,128)(2,1)S(1)} all-gather(bf16[256,128]{1,0:T(8,128)(2,1)S(1)} %copy.63), channel_id=1, replica_groups=mesh['rep'=8,'shard'=4] {'rep'}, dimensions={1}, use_global_device_ids=true | all-gather | bytes 589824 | tf_op jit(solution)/shard_map/all_gather | solution.py:98
  761.6 15.7 %all-gather.34.cloned.1.call-done = bf16[656,1024]{1,0:T(8,128)(2,1)} async-done(((bf16[656,128]{1,0:T(8,128)(2,1)}), bf16[656,1024]{1,0:T(8,128)(2,1)}) %all-gather.34.cloned.1.call-update) | async-done | bytes 1343504 | tf_op jit(solution)/shard_map/all_gather | solution.py:98
  780.4 43.5 %all-gather.24.cloned.1.call-done = bf16[256,3072]{1,0:T(8,128)(2,1)} async-done(((bf16[256,384]{1,0:T(8,128)(2,1)}), bf16[256,3072]{1,0:T(8,128)(2,1)}) %all-gather.24.cloned.1.call-update) | async-done | bytes 1572880 | tf_op jit(solution)/shard_map/all_gather | solution.py:95
  827.3 52.4 %all-gather.30.cloned.1.call-done = bf16[256,5248]{0,1:T(8,128)(2,1)} async-done(((bf16[256,656]{0,1:T(8,128)(2,1)}), bf16[256,5248]{0,1:T(8,128)(2,1)}) %all-gather.30.cloned.1.call-update) | async-done | bytes 2686992 | tf_op jit(solution)/shard_map/all_gather | solution.py:95
  879.7 5.0 copy.58
  (213 shorter events, 103.8 us)
Async XLA Ops:
  7.2 51.5 %all-gather.14.cloned.1.call-start = ((), (), s32[]{:S(2)}) async-start(), calls=%async_computation.8 | async-start | bytes 7864320 | tf_op jit(solution)/shard_map/all_gather | solution.py:124
  7.9 88.8 %all-gather.16.cloned.1.call-start = ((), (), s32[]{:S(2)}) async-start(), calls=%async_computation.9 | async-start | bytes 2621440 | tf_op jit(solution)/shard_map/all_gather | solution.py:125
  8.7 9.0 %copy-start.37 = (s32[1,1024]{1,0:T(1,128)S(1)}, s32[1,1024]{1,0:T(1,128)}, u32[]{:S(2)}) copy-start(s32[1,1024]{1,0:T(1,128)} %param.14) | copy-start | bytes 12292
  8.7 150.0 %all-gather.18.cloned.1.call-start = ((), (), s32[]{:S(2)}) async-start(), calls=%async_computation.10 | async-start | bytes 13434880 | tf_op jit(solution)/shard_map/all_gather | solution.py:170
  9.4 191.9 %all-gather.20.cloned.1.call-start = ((), (), s32[]{:S(2)}) async-start(), calls=%async_computation.11 | async-start | bytes 6717440 | tf_op jit(solution)/shard_map/all_gather | solution.py:171
  10.0 307.1 %all-gather.32.cloned.1.call-start = ((), (), s32[]{:S(2)}) async-start(), calls=%async_computation.18 | async-start | bytes 2621440 | tf_op jit(solution)/shard_map/all_gather | solution.py:254
  10.6 335.8 %all-gather.22.cloned.1.call-start = ((), (), s32[]{:S(2)}) async-start(), calls=%async_computation.12 | async-start | bytes 7864320 | tf_op jit(solution)/shard_map/all_gather | solution.py:251
  10.8 52.4 %copy-start.33 = (f32[256]{0:T(256)}, f32[256]{0:T(256)S(1)}, u32[]{:S(2)}) copy-start(f32[256]{0:T(256)S(1)} %broadcast_multiply_fusion.5) | copy-start | bytes 3076
  11.2 52.1 %copy-start.35 = (f32[256]{0:T(256)}, f32[256]{0:T(256)S(1)}, u32[]{:S(2)}) copy-start(f32[256]{0:T(256)S(1)} %add_rsqrt_fusion.1) | copy-start | bytes 3076
  17.2 46.1 %copy-start.30 = (f32[4,1,256]{2,1,0:T(1,128)}, f32[4,1,256]{2,1,0:T(1,128)S(1)}, u32[]{:S(2)}) copy-start(f32[4,1,256]{2,1,0:T(1,128)S(1)} %convert_element_type.138) | copy-start | bytes 12292
  17.5 45.8 %copy-start.18 = (bf16[256,1024]{1,0:T(8,128)(2,1)}, bf16[256,1024]{1,0:T(8,128)(2,1)S(1)}, u32[]{:S(2)}) copy-start(bf16[256,1024]{1,0:T(8,128)(2,1)S(1)} %fusion.19) | copy-start | bytes 1572868
  17.7 51.3 %copy-start.28 = (f32[256,32]{0,1:T(8,128)}, f32[256,32]{0,1:T(8,128)S(1)}, u32[]{:S(2)}) copy-start(f32[256,32]{0,1:T(8,128)S(1)} %get-tuple-element.93) | copy-start | bytes 98308
  71.5 14.2 %collective-permute-start = (bf16[2,64,1024]{2,1,0:T(8,128)(2,1)S(1)}, bf16[2,64,1024]{2,1,0:T(8,128)(2,1)S(1)}, u32[]{:S(2)}, u32[]{:S(2)}) collective-permute-start(bf16[2,64,1024]{2,1,0:T(8,128)(2,1)S(1)} %get-tuple-element.86), channel_id=1, source_target_pairs={{0,1},{1,2},{2,3},{4,5},{5,6},{6,7},{8,9},{9,10},{10,11},{12,13},{... | collective-permute-start | bytes 786440 | tf_op jit(solution)/shard_map/ppermute | solution.py:25
  73.7 12.1 %collective-permute-start.1 = (bf16[2,64,1024]{2,1,0:T(8,128)(2,1)S(1)}, bf16[2,64,1024]{2,1,0:T(8,128)(2,1)S(1)}, u32[]{:S(2)}, u32[]{:S(2)}) collective-permute-start(bf16[2,64,1024]{2,1,0:T(8,128)(2,1)S(1)} %get-tuple-element.87), channel_id=1, source_target_pairs={{1,0},{2,1},{3,2},{5,4},{6,5},{7,6},{9,8},{10,9},{11,10},{13,12},{... | collective-permute-start | bytes 786440 | tf_op jit(solution)/shard_map/ppermute | solution.py:26
  100.0 67.4 %copy-start.8 = (bf16[256,1024]{1,0:T(8,128)(2,1)}, bf16[256,1024]{1,0:T(8,128)(2,1)S(1)}, u32[]{:S(2)}) copy-start(bf16[256,1024]{1,0:T(8,128)(2,1)S(1)} %multiply_convert_fusion.3) | copy-start | bytes 1572868
  100.0 101.3 %copy-start.26 = (bf16[256,1024]{1,0:T(8,128)(2,1)S(1)}, bf16[256,1024]{1,0:T(8,128)(2,1)}, u32[]{:S(2)}) copy-start(bf16[256,1024]{1,0:T(8,128)(2,1)} %param.21) | copy-start | bytes 1572868
  201.3 11.2 %copy-start.1 = (f32[256,5248]{1,0:T(8,128)S(1)}, f32[256,5248]{1,0:T(8,128)}, u32[]{:S(2)}) copy-start(f32[256,5248]{1,0:T(8,128)} %fusion.50) | copy-start | bytes 16121860
  225.9 10.2 %slice-start = ((s8[6291456]{0:T(1024)(128)(4,1)}), s8[2097152]{0:T(1024)(128)(4,1)S(1)}, s32[]{:S(2)}) async-start(s8[6291456]{0:T(1024)(128)(4,1)} %bitcast.89), calls=%async_computation.23 | async-start | bytes 4194304
  242.1 6.4 collective-permute-start.2
  244.4 4.1 collective-permute-start.3
  263.3 8.8 copy-start.29
  276.0 149.6 %all-gather.28.cloned.1.call-start = ((), (), s32[]{:S(2)}) async-start(), calls=%async_computation.15 | async-start | bytes 13434880 | tf_op jit(solution)/shard_map/all_gather | solution.py:253
  276.8 179.5 %all-gather.26.cloned.1.call-start = ((), (), s32[]{:S(2)}) async-start(), calls=%async_computation.14 | async-start | bytes 2621440 | tf_op jit(solution)/shard_map/all_gather | solution.py:252
  277.5 247.0 %reduce-scatter.17.cloned.1.call-start = ((), (), s32[]{:S(2)}) async-start(), calls=%async_computation.22 | async-start | bytes 1769472
  324.4 268.2 %reduce-scatter.13.cloned.1.call-start = ((), (), s32[]{:S(2)}) async-start(), calls=%async_computation.20 | async-start | bytes 1769472
  354.9 311.6 %reduce-scatter.11.cloned.1.call-start = ((), (), s32[]{:S(2)}) async-start(), calls=%async_computation.16 | async-start | bytes 3022848 | tf_op jit(solution)/shard_map/reduce_scatter | solution.py:87
  435.7 295.5 %reduce-scatter.15.cloned.1.call-start = ((), (), s32[]{:S(2)}) async-start(), calls=%async_computation.21 | async-start | bytes 589824
  456.3 210.2 %copy-start.41 = (u32[32]{0:T(128)S(1)}, u32[32]{0:T(128)}, u32[]{:S(2)}) copy-start(u32[32]{0:T(128)} %constant.167) | copy-start | bytes 388
  459.7 317.6 %all-gather.34.cloned.1.call-start = ((), (), s32[]{:S(2)}) async-start(), calls=%async_computation.19 | async-start | bytes 1511424 | tf_op jit(solution)/shard_map/all_gather | solution.py:98
  526.3 297.5 %all-gather.24.cloned.1.call-start = ((), (), s32[]{:S(2)}) async-start(), calls=%async_computation.13 | async-start | bytes 1769472 | tf_op jit(solution)/shard_map/all_gather | solution.py:95
  594.4 285.3 %all-gather.30.cloned.1.call-start = ((), (), s32[]{:S(2)}) async-start(), calls=%async_computation.17 | async-start | bytes 3022848 | tf_op jit(solution)/shard_map/all_gather | solution.py:95
  673.0 31.7 %copy-start.11 = (f32[256,1024]{1,0:T(8,128)S(1)}, f32[256,1024]{1,0:T(8,128)}, u32[]{:S(2)}) copy-start(f32[256,1024]{1,0:T(8,128)} %get-tuple-element.67) | copy-start | bytes 3145732
  (31 other events, 103.7 us)
Sparse Core Ops, SparseCore 0:
  9.6 49.0 all-gather.13
  60.2 23.7 all-gather.15
  85.6 72.9 all-gather.17
  160.1 41.1 all-gather.19
  202.7 22.5 all-gather.31
  276.2 70.2 all-gather.21
  348.6 77.0 all-gather.27
  427.8 28.4 all-gather.25
  459.7 64.7 reduce-scatter.16
  528.8 63.8 reduce-scatter.12
  596.8 69.6 reduce-scatter.10
  670.2 60.9 reduce-scatter.14
  733.4 43.7 all-gather.33
  779.9 43.9 all-gather.23
  826.1 53.5 all-gather.29
where the time goes:
time: 898 us; the launch traced here: 891 us
  waiting for transfers between devices  538 us (60%)
  blocking collectives  159 us (18%)
  matrix products  88.3 us (10%)
  local copies, waits for them, and re-layouts  51.3 us (6%)
  other arithmetic  31.2 us (3%)
  between operations  15.7 us (2%)
    unnamed x18, waiting for transfers between devices  161 us
    all_gather x2, waiting for transfers between devices, replica_total(): lax.all_gather(first_share.astype(jnp.bfloat16), 'rep', axis=1, tiled=True)  95.9 us
    reduce_scatter x1, waiting for transfers between devices, replica_total(): lax.psum_scatter(first_part.astype(jnp.bfloat16), 'rep', scatter_dimensio...  71.8 us
    all_gather x1, waiting for transfers between devices, shards(): lax.all_gather(w_in, 'shard', axis=0, tiled=True)  58.6 us
    all_gather x1, waiting for transfers between devices, shards(): lax.all_gather(grad_up, 'shard', axis=0, tiled=True)  53.9 us
    all_gather x1, waiting for transfers between devices, shards(): lax.all_gather(w_qkv, 'shard', axis=0, tiled=True)  40.9 us
    all_to_all x1, blocking collectives, shards(): lax.all_to_all(act_low, 'shard', split_axis=1, concat_axis=0, tiled=True)  36.7 us
    all_gather x1, waiting for transfers between devices, shards(): lax.all_gather(w_down, 'shard', axis=0, tiled=True)  33.8 us
  transfers between devices with their start and end apart: 19, of which 13 were waited for; matrix products, arithmetic and copies ran while one was open for 18% of the time, Pallas kernels for 0%

commit v1 on v0

v1 whole, which is shorter than its diff:
```python
import math

import jax
import jax.numpy as jnp
from jax import lax
from jax.experimental import pallas as pl
from jax.experimental.pallas import tpu as pltpu
from jax.sharding import PartitionSpec as P

HEADS = 16
HEAD_DIM = 64
FF = 2624
HALF = 64
QB = 128

norm_epsilon = 1e-05
rope_base = 10000.0
masked_score = -1e30

F32 = jnp.float32
BF16 = jnp.bfloat16


def bit_of(axis, bit):
    return (lax.axis_index(axis) >> bit) & 1


def swap(x, axis, bit):
    size = lax.axis_size(axis)
    return lax.ppermute(x, axis, [(i, i ^ (1 << bit)) for i in range(size)])


def bits_of(axis):
    return lax.axis_size(axis).bit_length() - 1


def pick(x, index, dim):
    return lax.dynamic_index_in_dim(x, index, dim, keepdims=False)


def pair(mine, other, bit, dim):
    return jnp.where(bit == 0, jnp.stack([mine, other], dim), jnp.stack([other, mine], dim))


def gather_blocks(x, axis):
    count = bits_of(axis)
    shape = x.shape
    for step, bit in enumerate(reversed(range(count))):
        x = pair(x, swap(x, axis, bit), bit_of(axis, bit), step)
    return x.reshape((1 << count,) + shape)


def scatter_sum(x, axis):
    count = bits_of(axis)
    x = x.reshape((2,) * count + x.shape[1:])
    for bit in range(count):
        dim = count - 1 - bit
        b = bit_of(axis, bit)
        got = swap(pick(x, 1 - b, dim).astype(BF16), axis, bit)
        x = pick(x, b, dim).astype(F32) + got.astype(F32)
    return x


def all_to_all_blocks(x, axis):
    count = bits_of(axis)
    shape = x.shape
    x = x.reshape((2,) * count + shape[1:])
    for dim, bit in enumerate(reversed(range(count))):
        b = bit_of(axis, bit)
        got = swap(pick(x, 1 - b, dim), axis, bit)
        x = pair(pick(x, b, dim), got, b, dim)
    return x.reshape(shape)


def replica_scatter(x, order):
    left = list(reversed(range(bits_of("rep"))))
    x = x.reshape((2,) * len(left) + x.shape[1:])
    for bit in order:
        dim = left.index(bit)
        b = bit_of("rep", bit)
        got = swap(pick(x, 1 - b, dim), "rep", bit)
        x = (pick(x, b, dim).astype(F32) + got.astype(F32)).astype(BF16)
        left.remove(bit)
    return x


def replica_gather(x, order):
    shape = x.shape
    have = []
    for bit in reversed(order):
        have = sorted(have + [bit], reverse=True)
        x = pair(x, swap(x, "rep", bit), bit_of("rep", bit), have.index(bit))
    return x.reshape((1 << len(order),) + shape)


def partner(x):
    width = x.shape[-1]
    lane = lax.broadcasted_iota(jnp.int32, x.shape, 1)
    front = (lane % HEAD_DIM) < HEAD_DIM // 2
    return jnp.where(
        front,
        pltpu.roll(x, width - HEAD_DIM // 2, 1),
        pltpu.roll(x, HEAD_DIM // 2, 1),
    )


def head_masks(heads, width):
    lane = lax.broadcasted_iota(jnp.int32, (QB, width), 1) // HEAD_DIM
    return [lane == h for h in range(heads)]


def stack_heads(x, masks):
    x = x.astype(F32)
    return jnp.concatenate([jnp.where(m, x, 0.0) for m in masks], axis=0).astype(BF16)


def merge_heads(x, masks):
    total = None
    for h, m in enumerate(masks):
        part = jnp.where(m, x[h * QB : (h + 1) * QB], 0.0)
        total = part if total is None else total + part
    return total


def window_bias(ids_q, ids_k):
    row = lax.broadcasted_iota(jnp.int32, (QB, QB + 2 * HALF), 0)
    col = lax.broadcasted_iota(jnp.int32, (QB, QB + 2 * HALF), 1)
    ids_q = jnp.concatenate([ids_q] * ((QB + 2 * HALF) // 128), axis=1)
    allowed = (col >= row) & (col <= row + 2 * HALF) & (ids_q == ids_k)
    return jnp.where(allowed, 0.0, masked_score)


def block_probs(stacked_q, keys, bias, heads):
    scores = lax.dot_general(
        stacked_q, keys, (((1,), (1,)), ((), ())), preferred_element_type=F32
    )
    rows, cols = scores.shape
    scores = (scores.reshape(heads, QB, cols) + bias[None]).reshape(rows, cols)
    weights = jnp.exp(scores - jnp.max(scores, axis=-1, keepdims=True))
    return weights * (1.0 / jnp.sum(weights, axis=-1, keepdims=True))


def attention_kernel(
    heads, width, qkv_ref, cos_ref, sin_ref, idq_ref, idk_ref, q_ref, k_ref, v_ref, out_ref
):
    seq = qkv_ref.shape[0]
    edge = jnp.zeros((HALF, width), BF16)
    for ref in (k_ref, v_ref):
        ref[0:HALF, :] = edge
        ref[seq + HALF : seq + 2 * HALF, :] = edge

    def prepare(i, carry):
        rows = pl.ds(pl.multiple_of(i * QB, QB), QB)
        shifted = pl.ds(pl.multiple_of(i * QB + HALF, HALF), QB)
        cos, sin = cos_ref[rows, :], sin_ref[rows, :]
        q = qkv_ref[rows, 0:width]
        k = qkv_ref[rows, width : 2 * width]
        rotated = (q * cos + partner(q) * sin).astype(BF16)
        q_ref[rows, :] = (rotated.astype(F32) * (1.0 / math.sqrt(HEAD_DIM))).astype(BF16)
        k_ref[shifted, :] = (k * cos + partner(k) * sin).astype(BF16)
        v_ref[shifted, :] = qkv_ref[rows, 2 * width : 3 * width].astype(BF16)
        return carry

    lax.fori_loop(0, seq // QB, prepare, 0)
    masks = head_masks(heads, width)

    def attend(i, carry):
        rows = pl.ds(pl.multiple_of(i * QB, QB), QB)
        window = pl.ds(pl.multiple_of(i * QB, QB), QB + 2 * HALF)
        bias = window_bias(idq_ref[rows, :], idk_ref[0:1, window])
        probs = block_probs(stack_heads(q_ref[rows, :], masks), k_ref[window, :], bias, heads)
        mixed = jnp.dot(probs.astype(BF16), v_ref[window, :], preferred_element_type=F32)
        out_ref[rows, :] = merge_heads(mixed, masks).astype(BF16)
        return carry

    lax.fori_loop(0, seq // QB, attend, 0)


def attention_back_kernel(
    heads, width, q_ref, k_ref, v_ref, da_ref, cos_ref, sin_ref, idq_ref, idk_ref, out_ref, dk, dv
):
    seq = q_ref.shape[0]
    dk[...] = jnp.zeros_like(dk)
    dv[...] = jnp.zeros_like(dv)
    masks = head_masks(heads, width)

    def back(i, carry):
        rows = pl.ds(pl.multiple_of(i * QB, QB), QB)
        window = pl.ds(pl.multiple_of(i * QB, QB), QB + 2 * HALF)
        bias = window_bias(idq_ref[rows, :], idk_ref[0:1, window])
        queries = stack_heads(q_ref[rows, :], masks)
        keys = k_ref[window, :]
        probs = block_probs(queries, keys, bias, heads)
        grads = stack_heads(da_ref[rows, :], masks)
        dprobs = lax.dot_general(
            grads, v_ref[window, :], (((1,), (1,)), ((), ())), preferred_element_type=F32
        )
        delta = jnp.sum(probs * dprobs, axis=-1, keepdims=True)
        dscores = (probs * (dprobs - delta)).astype(BF16)
        dq = merge_heads(jnp.dot(dscores, keys, preferred_element_type=F32), masks)
        dq = dq * (1.0 / math.sqrt(HEAD_DIM))
        cos, sin = cos_ref[rows, :], sin_ref[rows, :]
        out_ref[rows, 0:width] = (dq * cos - partner(dq) * sin).astype(BF16)
        dk[window, :] += lax.dot_general(
            dscores, queries, (((0,), (0,)), ((), ())), preferred_element_type=F32
        )
        dv[window, :] += lax.dot_general(
            probs.astype(BF16), grads, (((0,), (0,)), ((), ())), preferred_element_type=F32
        )
        return carry

    lax.fori_loop(0, seq // QB, back, 0)

    def finish(i, carry):
        rows = pl.ds(pl.multiple_of(i * QB, QB), QB)
        shifted = pl.ds(pl.multiple_of(i * QB + HALF, HALF), QB)
        cos, sin = cos_ref[rows, :], sin_ref[rows, :]
        g = dk[shifted, :]
        out_ref[rows, width : 2 * width] = (g * cos - partner(g) * sin).astype(BF16)
        out_ref[rows, 2 * width : 3 * width] = dv[shifted, :].astype(BF16)
        return carry

    lax.fori_loop(0, seq // QB, finish, 0)


def attention(qkv, tables, heads, width):
    seq = qkv.shape[0]
    shape = jax.ShapeDtypeStruct
    return pl.pallas_call(
        lambda *refs: attention_kernel(heads, width, *refs),
        out_shape=(
            shape((seq, width), BF16),
            shape((seq + 2 * HALF, width), BF16),
            shape((seq + 2 * HALF, width), BF16),
            shape((seq, width), BF16),
        ),
        compiler_params=pltpu.CompilerParams(vmem_limit_bytes=40 << 20),
        name="attention",
    )(qkv, *tables)


def attention_back(queries, keys, values, grads, tables, heads, width):
    seq = queries.shape[0]
    return pl.pallas_call(
        lambda *refs: attention_back_kernel(heads, width, *refs),
        out_shape=jax.ShapeDtypeStruct((seq, 3 * width), BF16),
        scratch_shapes=[pltpu.VMEM((seq + 2 * HALF, width), F32)] * 2,
        compiler_params=pltpu.CompilerParams(vmem_limit_bytes=40 << 20),
        name="attention_back",
    )(queries, keys, values, grads, *tables)


def layer_norm(values):
    centred = values - jnp.mean(values, axis=-1, keepdims=True)
    scale = lax.rsqrt(jnp.mean(centred * centred, axis=-1, keepdims=True) + norm_epsilon)
    return centred * scale, scale


def norm_backward(grad_hat, normed, scale):
    return (
        grad_hat
        - jnp.mean(grad_hat, axis=-1, keepdims=True)
        - normed * jnp.mean(grad_hat * normed, axis=-1, keepdims=True)
    ) * scale


def geglu(gate_part, linear_part):
    return jax.nn.gelu(gate_part, approximate=False) * linear_part


def dot(a, b, dims):
    return lax.dot_general(a, b, (dims, ((), ())), preferred_element_type=F32)


def shards(tokens, segment_ids, ln1_gain, w_qkv, w_out, ln2_gain, w_in, w_down, cotangent):
    n = lax.axis_size("shard")
    replicas = lax.axis_size("rep")
    me = lax.axis_index("shard")
    rows, model = tokens.shape
    seq = rows * n
    part = model // n
    ff = w_down.shape[0]
    heads = HEADS // n
    head_cols = heads * HEAD_DIM
    width = max(128, head_cols)

    gains = jnp.concatenate([ln1_gain, ln2_gain])
    gains = jnp.pad(gains, (0, model - 2 * part))[None]
    gains = jnp.pad(gains, ((0, 15), (0, 0)))
    first = gather_blocks(jnp.concatenate([tokens, gains]), "shard")
    all_tokens = first[:, :rows].reshape(seq, model)
    gain1 = first[:, rows, :part].reshape(model).astype(F32)
    gain2 = first[:, rows, part : 2 * part].reshape(model).astype(F32)

    qkv_to = w_qkv.reshape(part, 3, n, head_cols).transpose(2, 0, 1, 3)
    qkv_w = all_to_all_blocks(qkv_to.reshape(n, part, 3 * head_cols), "shard")
    qkv_w = qkv_w.reshape(model, 3 * head_cols)
    if width != head_cols:
        qkv_w = qkv_w.reshape(model, 3, head_cols)
        qkv_w = jnp.pad(qkv_w, ((0, 0), (0, 0), (0, width - head_cols)))
        qkv_w = qkv_w.reshape(model, 3 * width)
    out_w = gather_blocks(w_out, "shard").reshape(model, model)
    in_to = w_in.reshape(part, 2, n, ff).transpose(2, 0, 1, 3).reshape(n, part, 2 * ff)
    in_w = all_to_all_blocks(in_to, "shard").reshape(model, 2 * ff)
    cot = gather_blocks(cotangent, "shard").reshape(seq, model)

    lane = jnp.arange(width, dtype=jnp.int32) % HEAD_DIM
    half = HEAD_DIM // 2
    frequency = jnp.exp(
        -math.log(rope_base) * 2.0 * (lane % half).astype(F32) / HEAD_DIM
    )
    angles = jnp.arange(seq, dtype=F32)[:, None] * frequency[None, :]
    sign = jnp.where(lane < half, -1.0, 1.0)
    ids = segment_ids[0]
    tables = (
        jnp.cos(angles),
        jnp.sin(angles) * sign[None, :],
        jnp.broadcast_to(ids[:, None], (seq, 128)),
        jnp.pad(ids, (HALF, HALF), constant_values=-1)[None],
    )

    hat1, _ = layer_norm(all_tokens.astype(F32))
    normed1 = (hat1 * gain1).astype(BF16)
    qkv = dot(normed1, qkv_w, ((1,), (0,)))
    queries, keys, values, attended = attention(qkv, tables, heads, width)
    everyone = gather_blocks(attended[:, :head_cols], "shard")
    everyone = everyone.transpose(1, 0, 2).reshape(seq, model)
    hidden = all_tokens.astype(F32) + dot(everyone, out_w, ((1,), (0,)))
    hat2, scale2 = layer_norm(hidden)
    normed2 = (hat2 * gain2).astype(BF16)
    up = dot(normed2, in_w, ((1,), (0,)))
    act, geglu_pull = jax.vjp(geglu, up[:, :ff], up[:, ff:])
    act = act.astype(BF16)
    mlp = dot(act, w_down, ((1,), (0,)))
    mlp = scatter_sum(mlp.astype(BF16).reshape(n, rows, model), "shard")
    own = me * rows
    output = (lax.dynamic_slice_in_dim(hidden, own, rows) + mlp).astype(BF16)

    dact = dot(cot, w_down, ((1,), (1,)))
    dgate, dlin = geglu_pull(dact)
    dup = jnp.concatenate([dgate, dlin], axis=1).astype(BF16)
    dnormed2 = dot(dup, in_w, ((1,), (1,))).astype(BF16)
    dnormed2 = scatter_sum(dnormed2.reshape(n, rows, model), "shard")
    own_hat2 = lax.dynamic_slice_in_dim(hat2, own, rows)
    own_scale2 = lax.dynamic_slice_in_dim(scale2, own, rows)
    ln2_part = jnp.sum(dnormed2 * own_hat2, axis=0)
    dhidden = cotangent.astype(F32) + norm_backward(dnormed2 * gain2, own_hat2, own_scale2)
    dproj = gather_blocks(dhidden.astype(BF16), "shard").reshape(seq, model)
    down_grad = dot(act, cot, ((0,), (0,))).astype(BF16)
    in_grad = dot(normed2, dup, ((0,), (0,))).astype(BF16)

    out_grad = dot(attended[:, :head_cols], dproj, ((0,), (0,))).astype(BF16)
    dattended = dot(dproj, w_out, ((1,), (1,))).astype(BF16)
    if width != head_cols:
        dattended = jnp.pad(dattended, ((0, 0), (0, width - head_cols)))
    dqkv = attention_back(queries, keys, values, dattended, tables, heads, width)
    qkv_grad = dot(normed1, dqkv, ((0,), (0,))).astype(BF16)
    dnormed1 = dot(dqkv, qkv_w, ((1,), (1,))).astype(BF16)
    dnormed1 = scatter_sum(dnormed1.reshape(n, rows, model), "shard")
    own_hat1, own_scale1 = layer_norm(tokens.astype(F32))
    ln1_part = jnp.sum(dnormed1 * own_hat1, axis=0)
    input_grad = dhidden + norm_backward(dnormed1 * gain1, own_hat1, own_scale1)

    near = list(range(bits_of("rep")))
    far = near[1:] + near[:1]
    chunk = part // replicas

    def columns_total(grad, cols):
        grad = grad.reshape(n, replicas, chunk, cols).transpose(1, 0, 2, 3)
        grad = all_to_all_blocks(replica_scatter(grad, near), "shard")
        return replica_gather(grad, near).transpose(0, 2, 1, 3).reshape(part, n, cols)

    in_total = columns_total(in_grad, 2 * ff).reshape(part, n, 2, ff)
    in_total = in_total.transpose(0, 2, 1, 3).reshape(part, 2 * n * ff).astype(F32)

    def rows_total(grad):
        height, cols = grad.shape
        grad = grad.reshape(height, replicas, cols // replicas).transpose(1, 0, 2)
        grad = replica_gather(replica_scatter(grad, far), far)
        return grad.transpose(1, 0, 2).reshape(height, cols).astype(F32)

    down_total = rows_total(down_grad)
    out_total = rows_total(out_grad)
    if width != head_cols:
        qkv_grad = qkv_grad.reshape(model, 3, width)[:, :, :head_cols].reshape(model, 3 * head_cols)
    qkv_total = columns_total(qkv_grad, 3 * head_cols).reshape(part, n, 3, head_cols)
    qkv_total = qkv_total.transpose(0, 2, 1, 3).reshape(part, 3 * model).astype(F32)
    gain_parts = lax.psum(jnp.stack([ln1_part, ln2_part]), ("rep", "shard"))
    gain_parts = lax.dynamic_slice_in_dim(gain_parts, me * part, part, axis=1)
    return (
        output,
        input_grad,
        gain_parts[0],
        qkv_total,
        out_total,
        gain_parts[1],
        in_total,
        down_total,
    )


def solution(mesh):
    return jax.shard_map(
        shards,
        mesh=mesh,
        in_specs=(
            P(("rep", "shard"), None),
            P("rep", None),
            P("shard"),
            P("shard", None),
            P("shard", None),
            P("shard"),
            P("shard", None),
            P("shard", None),
            P(("rep", "shard"), None),
        ),
        out_specs=(
            P(("rep", "shard"), None),
            P(("rep", "shard"), None),
            P("shard"),
            P("shard", None),
            P("shard", None),
            P("shard"),
            P("shard", None),
            P("shard", None),
        ),
        check_vma=False,
    )
```

time: 898 us -> 542 us (0.60)
  waiting for transfers between devices: 538 us -> 188 us
  blocking collectives: 159 us -> 40.1 us
  local copies, waits for them, and re-layouts: 51.3 us -> 118 us
  matrix products: 88.3 us -> 38.1 us
  starting transfers between devices: 8.24 us -> 56.2 us
  other arithmetic: 31.2 us -> 70.7 us
  Pallas kernels: 0 us -> 17.4 us
  between operations: 15.7 us -> 2.25 us
    all_gather x11 -> x0, waiting for transfers between devices: 305 us -> none  [the longest x2 95.9 us: replica_total(): lax.all_gather(first_share.astype(jnp.bfloat16), 'rep', axis=1, tiled=True)]
    ppermute x4 -> x48, waiting for transfers between devices: 0.01 us -> 188 us  [swap(): return lax.ppermute(x, axis, [(i, i ^ 1 << bit) for i in range(size)])]
    unnamed x18 -> x0, waiting for transfers between devices: 161 us -> none
    all_to_all x4 -> x0, blocking collectives: 88.3 us -> none  [the longest x1 36.7 us: shards(): lax.all_to_all(act_low, 'shard', split_axis=1, concat_axis=0, tiled=True)]
    reduce_scatter x1 -> x0, waiting for transfers between devices: 71.8 us -> none  [replica_total(): lax.psum_scatter(first_part.astype(jnp.bfloat16), 'rep', scatter_dimensio...]
    dot_general x18 -> x12, matrix products: 88.3 us -> 38.1 us  [dot(): return lax.dot_general(a, b, (dims, ((), ())), preferred_element_type=F32)]
    ppermute x4 -> x48, starting transfers between devices: 7.07 us -> 56.2 us  [swap(): return lax.ppermute(x, axis, [(i, i ^ 1 << bit) for i in range(size)])]
    select_n x0 -> x41, other arithmetic: none -> 44.8 us  [the longest x40 44.8 us: pair(): jnp.where(bit == 0, jnp.stack([mine, other], dim), jnp.stack([other, mine...]
  transfers between devices with their start and end apart: 19 -> 48, of which waited for: 13 -> 22; matrix products, arithmetic and copies ran while one was open for 18% -> 30% of each run, Pallas kernels for 0% -> 3%
where the time goes in v1:
time: 542 us; the launch traced here: 531 us
  waiting for transfers between devices  188 us (35%)
  local copies, waits for them, and re-layouts  118 us (22%)
  other arithmetic  70.7 us (13%)
  starting transfers between devices  56.2 us (10%)
  blocking collectives  40.1 us (7%)
  matrix products  38.1 us (7%)
  Pallas kernels  17.4 us (3%)
    ppermute x48, waiting for transfers between devices, swap(): return lax.ppermute(x, axis, [(i, i ^ 1 << bit) for i in range(size)])  188 us
    ppermute x48, starting transfers between devices, swap(): return lax.ppermute(x, axis, [(i, i ^ 1 << bit) for i in range(size)])  56.2 us
    select_n x40, other arithmetic, pair(): jnp.where(bit == 0, jnp.stack([mine, other], dim), jnp.stack([other, mine...  44.8 us
    psum x1, blocking collectives, shards(): gain_parts = lax.psum(jnp.stack([ln1_part, ln2_part]), ('rep', 'shard'))  40.1 us
    dot_general x12, matrix products, dot(): return lax.dot_general(a, b, (dims, ((), ())), preferred_element_type=F32)  38.1 us
    unnamed x101, local copies, waits for them, and re-layouts  29.2 us
    select_n x8, local copies, waits for them, and re-layouts, pair(): jnp.where(bit == 0, jnp.stack([mine, other], dim), jnp.stack([other, mine...  26.9 us
    convert_element_type x4, local copies, waits for them, and re-layouts, shards(): in_total.transpose(0, 2, 1, 3).reshape(part, 2 * n * ff).astype(F32)  22.8 us
  transfers between devices with their start and end apart: 48, of which 22 were waited for; matrix products, arithmetic and copies ran while one was open for 30% of the time, Pallas kernels for 3%

profile of v1, /device:TPU:0, one launch (start us, length us, event | category | flops | bytes accessed | tf_op | source)
XLA Modules:
  0.0 531.2 jit_solution(12004314005289005925)
XLA Ops:
  12.6 4.5 copy.94
  32.5 24.3 %collective-permute-done = bf16[272,1024]{1,0:T(8,128)(2,1)} collective-permute-done((bf16[272,1024]{1,0:T(8,128)(2,1)}, bf16[272,1024]{1,0:T(8,128)(2,1)}, u32[]{:S(2)}, u32[]{:S(2)}) %collective-permute-start) | collective-permute-done | bytes 557088 | tf_op jit(solution)/shard_map/ppermute | solution.py:30
  64.4 20.4 %collective-permute-done.8 = bf16[2,256,1312]{1,2,0:T(8,128)(2,1)} collective-permute-done((bf16[2,256,1312]{1,2,0:T(8,128)(2,1)}, bf16[2,256,1312]{1,2,0:T(8,128)(2,1)}, u32[]{:S(2)}, u32[]{:S(2)}) %collective-permute-start.8) | collective-permute-done | bytes 1343520 | tf_op jit(solution)/shard_map/ppermute | solution.py:30
  100.1 8.3 %attention.1 = (bf16[1024,256]{1,0:T(8,128)(2,1)S(1)}, bf16[1152,256]{1,0:T(8,128)(2,1)S(1)}, bf16[1152,256]{1,0:T(8,128)(2,1)S(1)}, bf16[1024,256]{1,0:T(8,128)(2,1)}) custom-call(f32[1024,768]{1,0:T(8,128)S(1)} %fusion.70.refs_0_, f32[1024,256]{1,0:T(8,128)S(1)} %get-tuple-element.84.refs_1_.refs_4_, f32[1024,256]{1,0:T(8,128)S(1)} %get-tuple-element.83.refs_2_.refs_5_, ...), custom_call_target="tpu_custom_call" | custom-call | tf_op jit(solution)/shard_map/attention/pallas_call | solution.py:229
  114.7 10.9 %collective-permute-done.4 = bf16[1024,256]{1,0:T(8,128)(2,1)} collective-permute-done((bf16[1024,256]{1,0:T(8,128)(2,1)}, bf16[1024,256]{1,0:T(8,128)(2,1)}, u32[]{:S(2)}, u32[]{:S(2)}) %collective-permute-start.4) | collective-permute-done | bytes 524320 | tf_op jit(solution)/shard_map/ppermute | solution.py:30
  144.9 12.5 %copy.96 = bf16[2,2,256,1312]{2,1,0,3:T(2,128)(2,1)} copy(bf16[2,2,256,1312]{2,3,1,0:T(8,128)(2,1)S(1)} %maximum_select_fusion.2) | data formatting | bytes 5373952 | tf_op jit(solution)/shard_map/jit(_where)/select_n | solution.py:42
  157.4 7.1 %select_n.672 = bf16[1024,1312]{0,1:T(8,128)(2,1)} reshape(bf16[2,2,256,1312]{2,1,0,3:T(2,128)(2,1)} %copy.96) | data formatting | bytes 5373952 | tf_op jit(solution)/shard_map/jit(_where)/select_n | solution.py:42
  168.7 4.3 copy.92
  173.0 5.5 %fusion.69 = (f32[1024]{0:T(1024)S(1)}, f32[1024,1024]{1,0:T(8,128)S(1)}) fusion(bf16[1024,1024]{0,1:T(8,128)(2,1)} %bitcast.406, bf16[1024,1024]{1,0:T(8,128)(2,1)} %bitcast.405, bf16[4,256,1024]{2,1,0:T(8,128)(2,1)} %slice.28), kind=kOutput, calls=%fused_computation.233 | convolution fusion | flops 2150628352 | bytes 10489856 | tf_op jit(solution)/shard_map/dot_general | solution.py:272
  186.2 7.8 %add_convert_fusion = (bf16[1024,656]{0,1:T(8,128)(2,1)S(1)}, f32[1024,656]{0,1:T(8,128)S(1)}, f32[1024,656]{0,1:T(8,128)S(1)}) fusion(f32[1024,1312]{0,1:T(8,128)S(1)} %fusion.39, bf16[1024,1024]{1,0:T(8,128)(2,1)S(1)} %bitcast.403, bf16[656,1024]{1,0:T(8,128)(2,1)S(1)} %copy-done), kind=kOutput, calls=%fused_computation.28 | convolution fusion | flops 1424769024 | bytes 15532032 | tf_op jit(solution)/shard_map/dot_general | solution.py:272
  195.5 4.7 convolution_convert_fusion.1
  200.2 5.5 %convolution_convert_fusion = bf16[1024,1312]{0,1:T(8,128)(2,1)} fusion(bf16[1024,656]{0,1:T(8,128)(2,1)S(1)} %get-tuple-element.50, bf16[1024,656]{0,1:T(8,128)(2,1)S(1)} %get-tuple-element.48, f32[1024,1024]{1,0:T(8,128)S(1)} %subtract_multiply_fusion, f32[1024]{0:T(1024)S(1)} %bitcast.447), kind=kOutput, calls=%fused_computation.16 | convolution fusion | flops 2760278016 | bytes 9572352 | tf_op jit(solution)/shard_map/dot_general | solution.py:272
  208.7 4.5 copy.111
  221.8 10.3 %collective-permute-done.42 = bf16[2,2,656,128]{3,2,1,0:T(8,128)(2,1)S(1)} collective-permute-done((bf16[2,2,656,128]{3,2,1,0:T(8,128)(2,1)S(1)}, bf16[2,2,656,128]{3,2,1,0:T(8,128)(2,1)S(1)}, u32[]{:S(2)}, u32[]{:S(2)}) %collective-permute-start.42) | collective-permute-done | bytes 671776 | tf_op jit(solution)/shard_map/ppermute | solution.py:30
  236.1 14.0 %collective-permute-done.43 = bf16[2,656,128]{2,1,0:T(8,128)(2,1)S(1)} collective-permute-done((bf16[2,656,128]{2,1,0:T(8,128)(2,1)S(1)}, bf16[2,656,128]{2,1,0:T(8,128)(2,1)S(1)}, u32[]{:S(2)}, u32[]{:S(2)}) %collective-permute-start.43) | collective-permute-done | bytes 335904 | tf_op jit(solution)/shard_map/ppermute | solution.py:30
  268.2 13.6 %collective-permute-done.35 = bf16[2,4,32,1312]{3,2,1,0:T(8,128)(2,1)S(1)} collective-permute-done((bf16[2,4,32,1312]{3,2,1,0:T(8,128)(2,1)S(1)}, bf16[2,4,32,1312]{3,2,1,0:T(8,128)(2,1)S(1)}, u32[]{:S(2)}, u32[]{:S(2)}) %collective-permute-start.35) | collective-permute-done | bytes 671776 | tf_op jit(solution)/shard_map/ppermute | solution.py:30
  284.7 15.3 %collective-permute-done.36 = bf16[4,32,1312]{2,1,0:T(8,128)(2,1)S(1)} collective-permute-done((bf16[4,32,1312]{2,1,0:T(8,128)(2,1)S(1)}, bf16[4,32,1312]{2,1,0:T(8,128)(2,1)S(1)}, u32[]{:S(2)}, u32[]{:S(2)}) %collective-permute-start.36) | collective-permute-done | bytes 335904 | tf_op jit(solution)/shard_map/ppermute | solution.py:30
  309.9 7.2 %collective-permute-done.16 = bf16[256,1024]{1,0:T(8,128)(2,1)S(1)} collective-permute-done((bf16[256,1024]{1,0:T(8,128)(2,1)S(1)}, bf16[256,1024]{1,0:T(8,128)(2,1)S(1)}, u32[]{:S(2)}, u32[]{:S(2)}) %collective-permute-start.16) | collective-permute-done | bytes 524320 | tf_op jit(solution)/shard_map/ppermute | solution.py:30
  317.5 9.1 %collective-permute-done.47 = bf16[2,2,656,128]{3,2,1,0:T(8,128)(2,1)S(1)} collective-permute-done((bf16[2,2,656,128]{3,2,1,0:T(8,128)(2,1)S(1)}, bf16[2,2,656,128]{3,2,1,0:T(8,128)(2,1)S(1)}, u32[]{:S(2)}, u32[]{:S(2)}) %collective-permute-start.47) | collective-permute-done | bytes 671776 | tf_op jit(solution)/shard_map/ppermute | solution.py:30
  335.4 9.1 %attention_back.1 = bf16[1024,768]{1,0:T(8,128)(2,1)S(1)} custom-call(bf16[1024,256]{1,0:T(8,128)(2,1)S(1)} %copy-done.9, bf16[1152,256]{1,0:T(8,128)(2,1)S(1)} %copy-done.5, bf16[1152,256]{1,0:T(8,128)(2,1)S(1)} %copy-done.7, bf16[1024,256]{1,0:T(8,128)(2,1)S(1)} %convolution_convert_fusion.7.refs_3_, f32[1024,256]{1,0:T(8,128)S(1)} %get-tuple-element.84.refs_1_.refs_4_, ...), custom_call_target="tpu_custom_call" | custom-call | tf_op jit(solution)/shard_map/attention_back/pallas_call | solution.py:244
  346.5 6.4 %collective-permute-done.28 = bf16[2,2,256,128]{3,2,1,0:T(8,128)(2,1)S(1)} collective-permute-done((bf16[2,2,256,128]{3,2,1,0:T(8,128)(2,1)S(1)}, bf16[2,2,256,128]{3,2,1,0:T(8,128)(2,1)S(1)}, u32[]{:S(2)}, u32[]{:S(2)}) %collective-permute-start.28) | collective-permute-done | bytes 262176 | tf_op jit(solution)/shard_map/ppermute | solution.py:30
  356.7 4.2 collective-permute-done.29
  366.8 15.8 %collective-permute-done.31 = bf16[256,128]{1,0:T(8,128)(2,1)S(1)} collective-permute-done((bf16[256,128]{1,0:T(8,128)(2,1)S(1)}, bf16[256,128]{1,0:T(8,128)(2,1)S(1)}, u32[]{:S(2)}, u32[]{:S(2)}) %collective-permute-start.31) | collective-permute-done | bytes 65568 | tf_op jit(solution)/shard_map/ppermute | solution.py:30
  391.1 8.5 %collective-permute-done.21 = bf16[2,4,32,768]{3,2,0,1:T(8,128)(2,1)S(1)} collective-permute-done((bf16[2,4,32,768]{3,2,0,1:T(8,128)(2,1)S(1)}, bf16[2,4,32,768]{3,2,0,1:T(8,128)(2,1)S(1)}, u32[]{:S(2)}, u32[]{:S(2)}) %collective-permute-start.21) | collective-permute-done | bytes 393248 | tf_op jit(solution)/shard_map/ppermute | solution.py:30
  404.5 5.2 collective-permute-done.22
  412.7 4.1 collective-permute-done.23
  429.6 7.8 %collective-permute-done.25 = bf16[4,32,768]{2,1,0:T(8,128)(2,1)S(1)} collective-permute-done((bf16[4,32,768]{2,1,0:T(8,128)(2,1)S(1)}, bf16[4,32,768]{2,1,0:T(8,128)(2,1)S(1)}, u32[]{:S(2)}, u32[]{:S(2)}) %collective-permute-start.25) | collective-permute-done | bytes 196640 | tf_op jit(solution)/shard_map/ppermute | solution.py:30
  438.9 40.1 %psum.7 = f32[2,1024]{1,0:T(2,128)S(1)} all-reduce(f32[2,1024]{1,0:T(2,128)S(1)} %pad_maximum_fusion.6), channel_id=1, replica_groups=mesh['rep'=8,'shard'=4] {'rep','shard'}, use_global_device_ids=true, to_apply=%region_12.13 | all-reduce | flops 2048 | bytes 16384 | tf_op jit(solution)/shard_map/psum | solution.py:388
  490.9 9.4 %reshape.1418 = f32[256,4,2,656]{3,2,0,1:T(2,128)} reshape(f32[8,32,4,1312]{3,1,0,2:T(8,128)} %copy.122) | data formatting | bytes 10747904 | tf_op jit(solution)/shard_map/convert_element_type | solution.py:374
  500.3 10.0 %copy.123 = f32[256,2,4,656]{0,3,2,1:T(8,128)} copy(f32[256,2,4,656]{3,1,0,2:T(2,128)} %bitcast.350) | data formatting | bytes 10747904 | tf_op jit(solution)/shard_map/convert_element_type | solution.py:374
  510.4 6.0 %copy.129 = f32[256,5248]{1,0:T(8,128)} copy(f32[256,5248]{0,1:T(8,128)} %bitcast.352) | data formatting | bytes 10747904
  522.2 4.9 copy.107
  (331 shorter events, 207.5 us)
Async XLA Ops:
  0.6 26.0 %collective-permute-start.6 = (bf16[256,1024]{1,0:T(8,128)(2,1)}, bf16[256,1024]{1,0:T(8,128)(2,1)}, u32[]{:S(2)}, u32[]{:S(2)}) collective-permute-start(bf16[256,1024]{1,0:T(8,128)(2,1)} %param.13), channel_id=1, source_target_pairs={{0,2},{1,3},{2,0},{3,1},{4,6},{5,7},{6,4},{7,5},{8,10},{9,11},{10,... | collective-permute-start | bytes 1572872 | tf_op jit(solution)/shard_map/ppermute | solution.py:30
  3.7 25.8 %collective-permute-start.12 = (bf16[256,1024]{1,0:T(8,128)(2,1)}, bf16[256,1024]{1,0:T(8,128)(2,1)}, u32[]{:S(2)}, u32[]{:S(2)}) collective-permute-start(bf16[256,1024]{1,0:T(8,128)(2,1)} %param.17), channel_id=1, source_target_pairs={{0,2},{1,3},{2,0},{3,1},{4,6},{5,7},{6,4},{7,5},{8,10},{9,11},{10,... | collective-permute-start | bytes 1572872 | tf_op jit(solution)/shard_map/ppermute | solution.py:30
  9.1 50.1 %collective-permute-start.2 = (bf16[2,256,768]{1,2,0:T(8,128)(2,1)}, bf16[2,256,768]{1,2,0:T(8,128)(2,1)}, u32[]{:S(2)}, u32[]{:S(2)}) collective-permute-start(bf16[2,256,768]{1,2,0:T(8,128)(2,1)} %get-tuple-element.63), channel_id=1, source_target_pairs={{0,2},{1,3},{2,0},{3,1},{4,6},{5,7},{6,4},{7,5},{8,10},{9,11},{10,... | collective-permute-start | bytes 2359304 | tf_op jit(solution)/shard_map/ppermute | solution.py:30
  12.5 44.3 %collective-permute-start = (bf16[272,1024]{1,0:T(8,128)(2,1)}, bf16[272,1024]{1,0:T(8,128)(2,1)}, u32[]{:S(2)}, u32[]{:S(2)}) collective-permute-start(bf16[272,1024]{1,0:T(8,128)(2,1)} %get-tuple-element.68), channel_id=1, source_target_pairs={{0,2},{1,3},{2,0},{3,1},{4,6},{5,7},{6,4},{7,5},{8,10},{9,11},{10,... | collective-permute-start | bytes 1671176 | tf_op jit(solution)/shard_map/ppermute | solution.py:30
  20.7 64.1 %collective-permute-start.8 = (bf16[2,256,1312]{1,2,0:T(8,128)(2,1)}, bf16[2,256,1312]{1,2,0:T(8,128)(2,1)}, u32[]{:S(2)}, u32[]{:S(2)}) collective-permute-start(bf16[2,256,1312]{1,2,0:T(8,128)(2,1)} %get-tuple-element.57), channel_id=1, source_target_pairs={{0,2},{1,3},{2,0},{3,1},{4,6},{5,7},{6,4},{7,5},{8,10},{9,11},{10,... | collective-permute-start | bytes 4030472 | tf_op jit(solution)/shard_map/ppermute | solution.py:30
  29.4 101.0 %collective-permute-start.7 = (bf16[2,256,1024]{2,1,0:T(8,128)(2,1)}, bf16[2,256,1024]{2,1,0:T(8,128)(2,1)}, u32[]{:S(2)}, u32[]{:S(2)}) collective-permute-start(bf16[2,256,1024]{2,1,0:T(8,128)(2,1)} %maximum_select_fusion.19), channel_id=1, source_target_pairs={{0,1},{1,0},{2,3},{3,2},{4,5},{5,4},{6,7},{7,6},{8,9},{9,8},{10,11... | collective-permute-start | bytes 3145736 | tf_op jit(solution)/shard_map/ppermute | solution.py:30
  32.0 101.9 %collective-permute-start.13 = (bf16[2,256,1024]{2,1,0:T(8,128)(2,1)}, bf16[2,256,1024]{2,1,0:T(8,128)(2,1)}, u32[]{:S(2)}, u32[]{:S(2)}) collective-permute-start(bf16[2,256,1024]{2,1,0:T(8,128)(2,1)} %maximum_select_fusion.20), channel_id=1, source_target_pairs={{0,1},{1,0},{2,3},{3,2},{4,5},{5,4},{6,7},{7,6},{8,9},{9,8},{10,11... | collective-permute-start | bytes 3145736 | tf_op jit(solution)/shard_map/ppermute | solution.py:30
  59.2 33.4 %collective-permute-start.1 = (bf16[2,272,1024]{2,1,0:T(8,128)(2,1)}, bf16[2,272,1024]{2,1,0:T(8,128)(2,1)}, u32[]{:S(2)}, u32[]{:S(2)}) collective-permute-start(bf16[2,272,1024]{2,1,0:T(8,128)(2,1)} %maximum_select_fusion.15), channel_id=1, source_target_pairs={{0,1},{1,0},{2,3},{3,2},{4,5},{5,4},{6,7},{7,6},{8,9},{9,8},{10,11... | collective-permute-start | bytes 3342344 | tf_op jit(solution)/shard_map/ppermute | solution.py:30
  61.0 27.6 %collective-permute-start.3 = (bf16[2,256,768]{1,2,0:T(8,128)(2,1)S(1)}, bf16[2,256,768]{1,2,0:T(8,128)(2,1)S(1)}, u32[]{:S(2)}, u32[]{:S(2)}) collective-permute-start(bf16[2,256,768]{1,2,0:T(8,128)(2,1)S(1)} %get-tuple-element.61), channel_id=1, source_target_pairs={{0,1},{1,0},{2,3},{3,2},{4,5},{5,4},{6,7},{7,6},{8,9},{9,8},{10,11... | collective-permute-start | bytes 2359304 | tf_op jit(solution)/shard_map/ppermute | solution.py:30
  88.6 54.2 %collective-permute-start.9 = (bf16[2,256,1312]{1,2,0:T(8,128)(2,1)}, bf16[2,256,1312]{1,2,0:T(8,128)(2,1)}, u32[]{:S(2)}, u32[]{:S(2)}) collective-permute-start(bf16[2,256,1312]{1,2,0:T(8,128)(2,1)} %get-tuple-element.55), channel_id=1, source_target_pairs={{0,1},{1,0},{2,3},{3,2},{4,5},{5,4},{6,7},{7,6},{8,9},{9,8},{10,11... | collective-permute-start | bytes 4030472 | tf_op jit(solution)/shard_map/ppermute | solution.py:30
  128.5 36.0 %collective-permute-start.5 = (bf16[2,1024,256]{2,1,0:T(8,128)(2,1)}, bf16[2,1024,256]{2,1,0:T(8,128)(2,1)}, u32[]{:S(2)}, u32[]{:S(2)}) collective-permute-start(bf16[2,1024,256]{2,1,0:T(8,128)(2,1)} %maximum_select_fusion.17), channel_id=1, source_target_pairs={{0,1},{1,0},{2,3},{3,2},{4,5},{5,4},{6,7},{7,6},{8,9},{9,8},{10,11... | collective-permute-start | bytes 3145736 | tf_op jit(solution)/shard_map/ppermute | solution.py:30
  214.5 17.6 %collective-permute-start.42 = (bf16[2,2,656,128]{3,2,1,0:T(8,128)(2,1)S(1)}, bf16[2,2,656,128]{3,2,1,0:T(8,128)(2,1)S(1)}, u32[]{:S(2)}, u32[]{:S(2)}) collective-permute-start(bf16[2,2,656,128]{3,2,1,0:T(8,128)(2,1)S(1)} %dynamic-slice_bitcast_fusion.9), channel_id=1, source_target_pairs={{0,8},{4,12},{8,0},{12,4},{16,24},{20,28},{24,16},{28,20},{1,9},{5... | collective-permute-start | bytes 2015240 | tf_op jit(solution)/shard_map/ppermute | solution.py:30
  217.7 34.2 %collective-permute-start.14 = (bf16[2,256,1024]{2,1,0:T(8,128)(2,1)S(1)}, bf16[2,256,1024]{2,1,0:T(8,128)(2,1)S(1)}, u32[]{:S(2)}, u32[]{:S(2)}) collective-permute-start(bf16[2,256,1024]{2,1,0:T(8,128)(2,1)S(1)} %dynamic-slice_bitcast_fusion.3), channel_id=1, source_target_pairs={{0,1},{1,0},{2,3},{3,2},{4,5},{5,4},{6,7},{7,6},{8,9},{9,8},{10,11... | collective-permute-start | bytes 3145736 | tf_op jit(solution)/shard_map/ppermute | solution.py:30
  218.4 39.1 %collective-permute-start.34 = (bf16[2,2,4,32,1312]{4,3,2,1,0:T(8,128)(2,1)S(1)}, bf16[2,2,4,32,1312]{4,3,2,1,0:T(8,128)(2,1)S(1)}, u32[]{:S(2)}, u32[]{:S(2)}) collective-permute-start(bf16[2,2,4,32,1312]{4,3,2,1,0:T(8,128)(2,1)S(1)} %bitcast.421), channel_id=1, source_target_pairs={{0,4},{4,0},{8,12},{12,8},{16,20},{20,16},{24,28},{28,24},{1,5},{5... | collective-permute-start | bytes 4030472 | tf_op jit(solution)/shard_map/ppermute | solution.py:30
  232.4 17.8 %collective-permute-start.43 = (bf16[2,656,128]{2,1,0:T(8,128)(2,1)S(1)}, bf16[2,656,128]{2,1,0:T(8,128)(2,1)S(1)}, u32[]{:S(2)}, u32[]{:S(2)}) collective-permute-start(bf16[2,656,128]{2,1,0:T(8,128)(2,1)S(1)} %dynamic-slice_bitcast_fusion.12), channel_id=1, source_target_pairs={{0,16},{4,20},{8,24},{12,28},{16,0},{20,4},{24,8},{28,12},{1,17},{... | collective-permute-start | bytes 1007624 | tf_op jit(solution)/shard_map/ppermute | solution.py:30
  235.3 18.7 %collective-permute-start.10 = (bf16[2,256,1024]{2,1,0:T(8,128)(2,1)S(1)}, bf16[2,256,1024]{2,1,0:T(8,128)(2,1)S(1)}, u32[]{:S(2)}, u32[]{:S(2)}) collective-permute-start(bf16[2,256,1024]{2,1,0:T(8,128)(2,1)S(1)} %dynamic-slice_bitcast_fusion.4), channel_id=1, source_target_pairs={{0,1},{1,0},{2,3},{3,2},{4,5},{5,4},{6,7},{7,6},{8,9},{9,8},{10,11... | collective-permute-start | bytes 3145736 | tf_op jit(solution)/shard_map/ppermute | solution.py:30
  257.9 23.9 %collective-permute-start.35 = (bf16[2,4,32,1312]{3,2,1,0:T(8,128)(2,1)S(1)}, bf16[2,4,32,1312]{3,2,1,0:T(8,128)(2,1)S(1)}, u32[]{:S(2)}, u32[]{:S(2)}) collective-permute-start(bf16[2,4,32,1312]{3,2,1,0:T(8,128)(2,1)S(1)} %dynamic-slice_bitcast_fusion.8), channel_id=1, source_target_pairs={{0,8},{4,12},{8,0},{12,4},{16,24},{20,28},{24,16},{28,20},{1,9},{5... | collective-permute-start | bytes 2015240 | tf_op jit(solution)/shard_map/ppermute | solution.py:30
  259.5 47.9 %collective-permute-start.11 = (bf16[256,1024]{1,0:T(8,128)(2,1)S(1)}, bf16[256,1024]{1,0:T(8,128)(2,1)S(1)}, u32[]{:S(2)}, u32[]{:S(2)}) collective-permute-start(bf16[256,1024]{1,0:T(8,128)(2,1)S(1)} %fusion.44), channel_id=1, source_target_pairs={{0,2},{1,3},{2,0},{3,1},{4,6},{5,7},{6,4},{7,5},{8,10},{9,11},{10,... | collective-permute-start | bytes 1572872 | tf_op jit(solution)/shard_map/ppermute | solution.py:30
  261.3 42.3 %collective-permute-start.46 = (bf16[2,656,128]{2,1,0:T(8,128)(2,1)S(1)}, bf16[2,656,128]{2,1,0:T(8,128)(2,1)S(1)}, u32[]{:S(2)}, u32[]{:S(2)}) collective-permute-start(bf16[2,656,128]{2,1,0:T(8,128)(2,1)S(1)} %maximum_select_fusion.34), channel_id=1, source_target_pairs={{0,16},{4,20},{8,24},{12,28},{16,0},{20,4},{24,8},{28,12},{1,17},{... | collective-permute-start | bytes 1007624 | tf_op jit(solution)/shard_map/ppermute | solution.py:30
  282.0 18.0 %collective-permute-start.36 = (bf16[4,32,1312]{2,1,0:T(8,128)(2,1)S(1)}, bf16[4,32,1312]{2,1,0:T(8,128)(2,1)S(1)}, u32[]{:S(2)}, u32[]{:S(2)}) collective-permute-start(bf16[4,32,1312]{2,1,0:T(8,128)(2,1)S(1)} %dynamic-slice_bitcast_fusion.11), channel_id=1, source_target_pairs={{0,16},{4,20},{8,24},{12,28},{16,0},{20,4},{24,8},{28,12},{1,17},{... | collective-permute-start | bytes 1007624 | tf_op jit(solution)/shard_map/ppermute | solution.py:30
  303.8 22.8 %collective-permute-start.47 = (bf16[2,2,656,128]{3,2,1,0:T(8,128)(2,1)S(1)}, bf16[2,2,656,128]{3,2,1,0:T(8,128)(2,1)S(1)}, u32[]{:S(2)}, u32[]{:S(2)}) collective-permute-start(bf16[2,2,656,128]{3,2,1,0:T(8,128)(2,1)S(1)} %maximum_select_fusion.27), channel_id=1, source_target_pairs={{0,8},{4,12},{8,0},{12,4},{16,24},{20,28},{24,16},{28,20},{1,9},{5... | collective-permute-start | bytes 2015240 | tf_op jit(solution)/shard_map/ppermute | solution.py:30
  309.8 19.5 %collective-permute-start.39 = (bf16[4,32,1312]{2,1,0:T(8,128)(2,1)S(1)}, bf16[4,32,1312]{2,1,0:T(8,128)(2,1)S(1)}, u32[]{:S(2)}, u32[]{:S(2)}) collective-permute-start(bf16[4,32,1312]{2,1,0:T(8,128)(2,1)S(1)} %bitcast.359), channel_id=1, source_target_pairs={{0,16},{4,20},{8,24},{12,28},{16,0},{20,4},{24,8},{28,12},{1,17},{... | collective-permute-start | bytes 1007624 | tf_op jit(solution)/shard_map/ppermute | solution.py:30
  329.5 53.3 %collective-permute-start.40 = (bf16[2,4,32,1312]{3,2,1,0:T(8,128)(2,1)S(1)}, bf16[2,4,32,1312]{3,2,1,0:T(8,128)(2,1)S(1)}, u32[]{:S(2)}, u32[]{:S(2)}) collective-permute-start(bf16[2,4,32,1312]{3,2,1,0:T(8,128)(2,1)S(1)} %maximum_select_fusion.25), channel_id=1, source_target_pairs={{0,8},{4,12},{8,0},{12,4},{16,24},{20,28},{24,16},{28,20},{1,9},{5... | collective-permute-start | bytes 2015240 | tf_op jit(solution)/shard_map/ppermute | solution.py:30
  333.5 19.4 %collective-permute-start.28 = (bf16[2,2,256,128]{3,2,1,0:T(8,128)(2,1)S(1)}, bf16[2,2,256,128]{3,2,1,0:T(8,128)(2,1)S(1)}, u32[]{:S(2)}, u32[]{:S(2)}) collective-permute-start(bf16[2,2,256,128]{3,2,1,0:T(8,128)(2,1)S(1)} %dynamic-slice_bitcast_fusion.13), channel_id=1, source_target_pairs={{0,8},{4,12},{8,0},{12,4},{16,24},{20,28},{24,16},{28,20},{1,9},{5... | collective-permute-start | bytes 786440 | tf_op jit(solution)/shard_map/ppermute | solution.py:30
  361.7 23.8 %collective-permute-start.20 = (bf16[2,2,4,32,768]{4,3,1,0,2:T(8,128)(2,1)S(1)}, bf16[2,2,4,32,768]{4,3,1,0,2:T(8,128)(2,1)S(1)}, u32[]{:S(2)}, u32[]{:S(2)}) collective-permute-start(bf16[2,2,4,32,768]{4,3,1,0,2:T(8,128)(2,1)S(1)} %dynamic-slice_bitcast_fusion.5), channel_id=1, source_target_pairs={{0,4},{4,0},{8,12},{12,8},{16,20},{20,16},{24,28},{28,24},{1,5},{5... | collective-permute-start | bytes 2359304 | tf_op jit(solution)/shard_map/ppermute | solution.py:30
  366.1 16.5 %collective-permute-start.31 = (bf16[256,128]{1,0:T(8,128)(2,1)S(1)}, bf16[256,128]{1,0:T(8,128)(2,1)S(1)}, u32[]{:S(2)}, u32[]{:S(2)}) collective-permute-start(bf16[256,128]{1,0:T(8,128)(2,1)S(1)} %fusion.52), channel_id=1, source_target_pairs={{0,4},{4,0},{8,12},{12,8},{16,20},{20,16},{24,28},{28,24},{1,5},{5... | collective-permute-start | bytes 196616 | tf_op jit(solution)/shard_map/ppermute | solution.py:30
  366.7 34.2 %collective-permute-start.18 = (bf16[2,256,1024]{2,1,0:T(8,128)(2,1)S(1)}, bf16[2,256,1024]{2,1,0:T(8,128)(2,1)S(1)}, u32[]{:S(2)}, u32[]{:S(2)}) collective-permute-start(bf16[2,256,1024]{2,1,0:T(8,128)(2,1)S(1)} %dynamic-slice_bitcast_fusion.2), channel_id=1, source_target_pairs={{0,1},{1,0},{2,3},{3,2},{4,5},{5,4},{6,7},{7,6},{8,9},{9,8},{10,11... | collective-permute-start | bytes 3145736 | tf_op jit(solution)/shard_map/ppermute | solution.py:30
  384.2 100.8 %collective-permute-start.41 = (bf16[2,2,4,32,1312]{4,3,2,1,0:T(8,128)(2,1)}, bf16[2,2,4,32,1312]{4,3,2,1,0:T(8,128)(2,1)}, u32[]{:S(2)}, u32[]{:S(2)}) collective-permute-start(bf16[2,2,4,32,1312]{4,3,2,1,0:T(8,128)(2,1)} %maximum_select_fusion.12), channel_id=1, source_target_pairs={{0,4},{4,0},{8,12},{12,8},{16,20},{20,16},{24,28},{28,24},{1,5},{5... | collective-permute-start | bytes 4030472 | tf_op jit(solution)/shard_map/ppermute | solution.py:30
  391.0 26.0 %collective-permute-start.33 = (bf16[2,2,256,128]{3,2,1,0:T(8,128)(2,1)S(1)}, bf16[2,2,256,128]{3,2,1,0:T(8,128)(2,1)S(1)}, u32[]{:S(2)}, u32[]{:S(2)}) collective-permute-start(bf16[2,2,256,128]{3,2,1,0:T(8,128)(2,1)S(1)} %maximum_select_fusion.36), channel_id=1, source_target_pairs={{0,8},{4,12},{8,0},{12,4},{16,24},{20,28},{24,16},{28,20},{1,9},{5... | collective-permute-start | bytes 786440 | tf_op jit(solution)/shard_map/ppermute | solution.py:30
  402.2 25.4 %collective-permute-start.19 = (bf16[256,1024]{1,0:T(8,128)(2,1)}, bf16[256,1024]{1,0:T(8,128)(2,1)S(1)}, u32[]{:S(2)}, u32[]{:S(2)}) collective-permute-start(bf16[256,1024]{1,0:T(8,128)(2,1)} %fusion.46), channel_id=1, source_target_pairs={{0,2},{1,3},{2,0},{3,1},{4,6},{5,7},{6,4},{7,5},{8,10},{9,11},{10,... | collective-permute-start | bytes 1572872 | tf_op jit(solution)/shard_map/ppermute | solution.py:30
  438.9 42.9 %collective-permute-start.26 = (bf16[2,4,32,768]{3,2,1,0:T(8,128)(2,1)}, bf16[2,4,32,768]{3,2,1,0:T(8,128)(2,1)S(1)}, u32[]{:S(2)}, u32[]{:S(2)}) collective-permute-start(bf16[2,4,32,768]{3,2,1,0:T(8,128)(2,1)} %maximum_select_fusion.30), channel_id=1, source_target_pairs={{0,8},{4,12},{8,0},{12,4},{16,24},{20,28},{24,16},{28,20},{1,9},{5... | collective-permute-start | bytes 1179656 | tf_op jit(solution)/shard_map/ppermute | solution.py:30
  482.8 33.9 %collective-permute-start.27 = (bf16[2,2,4,32,768]{4,3,2,1,0:T(8,128)(2,1)}, bf16[2,2,4,32,768]{4,3,2,1,0:T(8,128)(2,1)}, u32[]{:S(2)}, u32[]{:S(2)}) collective-permute-start(bf16[2,2,4,32,768]{4,3,2,1,0:T(8,128)(2,1)} %maximum_select_fusion.23), channel_id=1, source_target_pairs={{0,4},{4,0},{8,12},{12,8},{16,20},{20,16},{24,28},{28,24},{1,5},{5... | collective-permute-start | bytes 2359304 | tf_op jit(solution)/shard_map/ppermute | solution.py:30
  (62 other events, 738.1 us)
